TPU v7x, 32 devices: a whole 2x2x4 slice. The times are simulated.
32 devices in a mesh: batch: 16 (over z, y, x), mp: 2 (over core).
Axes of the slice: x: 2, y: 2, z: 4, core: 2. Of those that a mesh axis runs over, the one named last changes fastest.
Arguments:
- hidden_in: bfloat16 [32, 1024, 768], P('batch', 'mp'), may hold values from -6 to 6
- memory_flags: int32 [32], P('batch'), may hold values 0 or 1
- memory_coeffs: bfloat16 [32, 256, 768], P('batch', 'mp'), may hold values from -6 to 6
- first_gain: float32 [768], replicated, may hold values from 0.25 to 1.75
- first_bias: float32 [768], replicated, may hold values from -1.5 to 1.5
- query_key_value_matrix: bfloat16 [768, 3, 768], P(None, None, 'mp'), may hold values from -0.21875 to 0.21875
- qv_bias: bfloat16 [2, 768], P(None, 'mp'), may hold values from -1.5 to 1.5
- memory_weight: bfloat16 [2, 12, 256], P(None, 'mp'), may hold values from -0.1875 to 0.1875
- memory_bias: bfloat16 [2, 12], P(None, 'mp'), may hold values from -1.5 to 1.5
- output_matrix: bfloat16 [768, 768], P('mp'), may hold values from -1.25 to 1.25
- out_bias: float32 [768], replicated, may hold values from -1.5 to 1.5
- second_gain: float32 [768], replicated, may hold values from 0.25 to 1.75
- second_bias: float32 [768], replicated, may hold values from -1.5 to 1.5
- up_matrix: bfloat16 [768, 3072], P(None, 'mp'), may hold values from -0.21875 to 0.21875
- up_bias_vector: bfloat16 [3072], P('mp'), may hold values from -1.5 to 1.5
- down_matrix: bfloat16 [3072, 768], P('mp'), may hold values from -0.109375 to 0.109375
- down_bias: float32 [768], replicated, may hold values from -1.5 to 1.5
- out_grad: bfloat16 [32, 1024, 768], P('batch', 'mp'), may hold values from -6 to 6
Outputs:
- block_out: bfloat16 [32, 1024, 768], P('batch', 'mp')
- input_grad: float32 [32, 1024, 768], P('batch', 'mp')
- coeff_grad: float32 [32, 256, 768], P('batch', 'mp')
- first_gain_grad: float32 [768], replicated
- first_bias_grad: float32 [768], replicated
- query_key_value_matrix_grad: float32 [768, 3, 768], P(None, None, 'mp')
- qv_bias_grad: float32 [2, 768], P(None, 'mp')
- memory_weight_grad: float32 [2, 12, 256], P(None, 'mp')
- memory_bias_grad: float32 [2, 12], P(None, 'mp')
- output_matrix_grad: float32 [768, 768], P('mp')
- out_bias_grad: float32 [768], replicated
- second_gain_grad: float32 [768], replicated
- second_bias_grad: float32 [768], replicated
- up_weight_grad: float32 [768, 3072], P(None, 'mp')
- up_bias_grad: float32 [3072], P('mp')
- down_weight_grad: float32 [3072, 768], P('mp')
- down_bias_grad: float32 [768], replicated
Inputs may be any that keep to these rules, and one draw needn't show every extreme that they name: memory_flags holds one flag per sequence.
All inputs are finite; a program needn't handle non-finite values. No bound on the sum of `memory_flags` on one device may be relied on, other than what follows from the above.
Results may differ from a plain program's by a relative error of at most 0.013.
The roundings to bfloat16 on the way count: a program that leaves them out, or rounds other values in their place, can miss the bound.
Values may be sent and summed in bfloat16 or wider, within the bound.
No kernel may reach another device: no remote copies, remote signals or barrier semaphores. Data moves between devices by JAX's collectives and lax.ppermute only.
A program may use at most 320 MiB of HBM per device.

v0:
```python
import math
import jax
import jax.numpy as jnp
from jax import lax
from jax.sharding import PartitionSpec as P

HD = 64


def product(form, left_side, right_side):
    return jnp.einsum(form, left_side, right_side, precision=lax.Precision.HIGHEST)


def matrix_multiply(form, left_side, right_side):
    return jnp.einsum(form, left_side, right_side, preferred_element_type=jnp.float32)


def norm_parts(values, gain_vec, bias_vec):
    row_mean = jnp.mean(values, axis=-1, keepdims=True)
    centred = values - row_mean
    row_var = jnp.mean(centred * centred, axis=-1, keepdims=True)
    inverse = lax.rsqrt(row_var + 1e-05)
    scaled = centred * inverse
    return (scaled * gain_vec + bias_vec, scaled, inverse)


def norm_back(grad_out, scaled, inverse, gain_vec):
    grad_scaled = grad_out * gain_vec
    first_mean = jnp.mean(grad_scaled, axis=-1, keepdims=True)
    second_mean = jnp.mean(grad_scaled * scaled, axis=-1, keepdims=True)
    return inverse * (grad_scaled - first_mean - scaled * second_mean)


def basis_weights(memory_scores, weight_pair, bias_pair):
    basis_count = memory_scores.shape[-1]
    mean_logit = product("slhn,hn->slh", memory_scores, weight_pair[0]) + bias_pair[0]
    var_logit = product("slhn,hn->slh", memory_scores, weight_pair[1]) + bias_pair[1]
    centre = jax.nn.sigmoid(mean_logit)
    spread = 0.05 * jax.nn.softplus(var_logit) + (8.0 / basis_count) ** 2
    places = (jnp.arange(basis_count, dtype=jnp.float32) + 0.5) / basis_count
    offset = places - centre[..., None]
    return (
        jnp.exp(-offset * offset / (2.0 * spread[..., None]))
        * lax.rsqrt(2.0 * math.pi * spread[..., None])
        / basis_count
    )


def causal_scores(block_queries, key_rows, start_row, end_row):
    scores = matrix_multiply("sqhd,skhd->shqk", block_queries, key_rows[:, :end_row]) * 0.125
    allowed = jnp.arange(end_row)[None, :] <= jnp.arange(start_row, end_row)[:, None]
    return jnp.where(allowed, scores, -1e30)


def attend_forward(
    norm_output,
    coeffs,
    flag_vec,
    query_key_value_matrix,
    qv_bias,
    memory_weight,
    memory_bias,
    output_matrix,
):
    seq_count, length, model_width = norm_output.shape
    local_width = query_key_value_matrix.shape[2]
    head_count = local_width // HD
    basis_count = coeffs.shape[1]
    head_shape = (seq_count, length, head_count, HD)
    bias_values = qv_bias.astype(jnp.float32)
    projected_rows = matrix_multiply("zam,mwr->zawr", norm_output, query_key_value_matrix)
    queries = (projected_rows[:, :, 0] + bias_values[0]).astype(jnp.bfloat16).reshape(head_shape)
    key_rows = projected_rows[:, :, 1].astype(jnp.bfloat16).reshape(head_shape)
    values = (projected_rows[:, :, 2] + bias_values[1]).astype(jnp.bfloat16).reshape(head_shape)
    memory = matrix_multiply("snd,dcf->sncf", coeffs, query_key_value_matrix[:, 1:]).astype(
        jnp.bfloat16
    )
    memory_keys = memory[:, :, 0].reshape(seq_count, basis_count, head_count, HD)
    memory_values = memory[:, :, 1].reshape(seq_count, basis_count, head_count, HD)
    block_rows = min(512, length)
    attended_parts = []
    total_parts = []
    for block_index in range(length // block_rows):
        start_row = block_index * block_rows
        end_row = start_row + block_rows
        scores = causal_scores(queries[:, start_row:end_row], key_rows, start_row, end_row)
        top_score = jnp.max(scores, axis=-1, keepdims=True)
        raised = jnp.exp(scores - top_score)
        denominator = jnp.sum(raised, axis=-1, keepdims=True)
        weights = (raised / denominator).astype(jnp.bfloat16)
        attended_parts.append(matrix_multiply("shqk,skhd->sqhd", weights, values[:, :end_row]))
        total_parts.append(top_score[..., 0] + jnp.log(denominator[..., 0]))
    attended = jnp.concatenate(attended_parts, axis=1)
    log_totals = jnp.concatenate(total_parts, axis=2)
    memory_scores = matrix_multiply("slhd,snhd->slhn", queries, memory_keys) * 0.125
    basis_mass = basis_weights(
        memory_scores, memory_weight.astype(jnp.float32), memory_bias.astype(jnp.float32)
    ).astype(jnp.bfloat16)
    recalled = matrix_multiply("slhn,snhd->slhd", basis_mass, memory_values)
    flag_values = flag_vec.astype(jnp.float32)[:, None, None, None]
    combined_heads = (
        (attended + flag_values * recalled)
        .astype(jnp.bfloat16)
        .reshape(seq_count, length, local_width)
    )
    residual_piece = matrix_multiply("hom,mu->hou", combined_heads, output_matrix)
    kept = (
        queries,
        key_rows,
        values,
        memory_keys,
        memory_values,
        memory_scores,
        basis_mass,
        combined_heads,
        log_totals,
    )
    return (residual_piece, kept)


def attend_backward(
    residual_grad,
    norm_output,
    coeffs,
    flag_vec,
    query_key_value_matrix,
    memory_weight,
    memory_bias,
    output_matrix,
    kept,
):
    (
        queries,
        key_rows,
        values,
        memory_keys,
        memory_values,
        memory_scores,
        basis_mass,
        combined_heads,
        log_totals,
    ) = kept
    seq_count, length, model_width = norm_output.shape
    local_width = query_key_value_matrix.shape[2]
    head_count = local_width // HD
    basis_count = coeffs.shape[1]
    output_matrix_grad = matrix_multiply("qro,qrv->ov", combined_heads, residual_grad)
    combined_heads_grad = matrix_multiply("kpo,wo->kpw", residual_grad, output_matrix).astype(
        jnp.bfloat16
    )
    combined_heads_grad = combined_heads_grad.reshape(seq_count, length, head_count, HD)
    recalled_grad = combined_heads_grad * flag_vec[:, None, None, None]
    basis_grad = matrix_multiply("slhd,snhd->slhn", recalled_grad, memory_values)
    mvalues_grad = matrix_multiply("slhn,slhd->snhd", basis_mass, recalled_grad)
    unused_mass, pullback = jax.vjp(
        basis_weights,
        memory_scores,
        memory_weight.astype(jnp.float32),
        memory_bias.astype(jnp.float32),
    )
    scores_grad, memory_weight_grad, memory_bias_grad = pullback(basis_grad)
    scores_grad = scores_grad.astype(jnp.bfloat16)
    query_grad = matrix_multiply("slhn,snhd->slhd", scores_grad, memory_keys) * 0.125
    mkeys_grad = matrix_multiply("slhn,slhd->snhd", scores_grad, queries) * 0.125
    key_grad = jnp.zeros(key_rows.shape, jnp.float32)
    value_grad = jnp.zeros(values.shape, jnp.float32)
    block_rows = min(512, length)
    query_parts = []
    for block_index in range(length // block_rows):
        start_row = block_index * block_rows
        end_row = start_row + block_rows
        block_queries = queries[:, start_row:end_row]
        block_grad = combined_heads_grad[:, start_row:end_row]
        scores = causal_scores(block_queries, key_rows, start_row, end_row)
        weights = jnp.exp(scores - log_totals[:, :, start_row:end_row, None])
        weights_grad = matrix_multiply("sqhd,skhd->shqk", block_grad, values[:, :end_row])
        inner_sum = jnp.sum(weights * weights_grad, axis=-1, keepdims=True)
        block_scores_grad = (weights * (weights_grad - inner_sum)).astype(jnp.bfloat16)
        query_parts.append(
            matrix_multiply("shqk,skhd->sqhd", block_scores_grad, key_rows[:, :end_row]) * 0.125
        )
        key_grad = key_grad.at[:, :end_row].add(
            matrix_multiply("shqk,sqhd->skhd", block_scores_grad, block_queries) * 0.125
        )
        value_grad = value_grad.at[:, :end_row].add(
            matrix_multiply("shqk,sqhd->skhd", weights.astype(jnp.bfloat16), block_grad)
        )
    query_grad = query_grad + jnp.concatenate(query_parts, axis=1)
    query_key_value_rows_grad = jnp.stack([query_grad, key_grad, value_grad], axis=2).astype(
        jnp.bfloat16
    )
    query_key_value_rows_grad = query_key_value_rows_grad.reshape(seq_count, length, 3, local_width)
    memory_grads = jnp.stack([mkeys_grad, mvalues_grad], axis=2).astype(jnp.bfloat16)
    memory_grads = memory_grads.reshape(seq_count, basis_count, 2, local_width)
    query_key_value_matrix_grad = matrix_multiply(
        "arh,arkq->hkq", norm_output, query_key_value_rows_grad
    )
    query_key_value_matrix_grad = query_key_value_matrix_grad.at[:, 1:].add(
        matrix_multiply("snd,sncf->dcf", coeffs, memory_grads)
    )
    qv_bias_grad = jnp.sum(query_key_value_rows_grad[:, :, 0::2].astype(jnp.float32), axis=(0, 1))
    norm_output_grad = matrix_multiply(
        "zwev,oev->zwo", query_key_value_rows_grad, query_key_value_matrix
    )
    coeffs_grad = matrix_multiply("sncf,dcf->snd", memory_grads, query_key_value_matrix[:, 1:])
    return (
        norm_output_grad,
        coeffs_grad,
        query_key_value_matrix_grad,
        qv_bias_grad,
        memory_weight_grad,
        memory_bias_grad,
        output_matrix_grad,
    )


def feed_forward(norm_output, up_matrix, up_bias_vector, down_matrix):
    input_rows = matrix_multiply("ahg,gm->ahm", norm_output, up_matrix) + up_bias_vector.astype(
        jnp.float32
    )
    gelu_output = jax.nn.gelu(input_rows, approximate=True).astype(jnp.bfloat16)
    return (matrix_multiply("hom,mu->hou", gelu_output, down_matrix), input_rows, gelu_output)


def feed_backward(gradient_rows, norm_output, up_matrix, down_matrix, input_rows, gelu_output):
    down_output_grad = matrix_multiply("qro,qrv->ov", gelu_output, gradient_rows)
    hidden_state_grad = matrix_multiply("kpo,wo->kpw", gradient_rows, down_matrix)
    unused_value, pullback = jax.vjp(
        lambda inputs: jax.nn.gelu(inputs, approximate=True), input_rows
    )
    (input_rows_grad,) = pullback(hidden_state_grad)
    input_rows_grad = input_rows_grad.astype(jnp.bfloat16)
    up_output_grad = matrix_multiply("orx,ora->xa", norm_output, input_rows_grad)
    upb_grad = jnp.sum(input_rows_grad.astype(jnp.float32), axis=(0, 1))
    norm_output_grad = matrix_multiply("iqg,kg->iqk", input_rows_grad, up_matrix)
    return (norm_output_grad, up_output_grad, upb_grad, down_output_grad)


def per_device(
    hidden_in,
    memory_flags,
    memory_coeffs,
    first_gain,
    first_bias,
    query_key_value_matrix,
    qv_bias,
    memory_weight,
    memory_bias,
    output_matrix,
    out_bias,
    second_gain,
    second_bias,
    up_matrix,
    up_bias_vector,
    down_matrix,
    down_bias,
    out_grad,
):
    hidden = hidden_in.astype(jnp.float32)
    flag_local = memory_flags.astype(jnp.bfloat16)
    normed_one, scaled_one, inverse_one = norm_parts(hidden, first_gain, first_bias)
    normed_one = normed_one.astype(jnp.bfloat16)
    normed_all, coeffs_all = (
        lax.all_gather(normed_one, "mp", axis=1, tiled=True),
        lax.all_gather(memory_coeffs, "mp", axis=1, tiled=True),
    )
    residual_piece, kept = attend_forward(
        normed_all,
        coeffs_all,
        flag_local,
        query_key_value_matrix,
        qv_bias,
        memory_weight,
        memory_bias,
        output_matrix,
    )
    branch_total = lax.psum_scatter(residual_piece, "mp", scatter_dimension=1, tiled=True)
    middle = hidden + (branch_total + out_bias)
    normed_two, scaled_two, inverse_two = norm_parts(middle, second_gain, second_bias)
    normed_two_all = lax.all_gather(normed_two.astype(jnp.bfloat16), "mp", axis=1, tiled=True)
    feed_part, input_rows, gelu_output = feed_forward(
        normed_two_all, up_matrix, up_bias_vector, down_matrix
    )
    feed_total = lax.psum_scatter(
        feed_part.astype(jnp.bfloat16), "mp", scatter_dimension=1, tiled=True
    ).astype(jnp.float32)
    block_out = (middle + feed_total + down_bias).astype(jnp.bfloat16)
    grad_all = lax.all_gather(out_grad, "mp", axis=1, tiled=True)
    normed_two_part, up_output_grad, upb_grad, down_output_grad = feed_backward(
        grad_all, normed_two_all, up_matrix, down_matrix, input_rows, gelu_output
    )
    normed_two_grad = lax.psum_scatter(normed_two_part, "mp", scatter_dimension=1, tiled=True)
    out_grad_values = out_grad.astype(jnp.float32)
    middle_grad = out_grad_values + norm_back(normed_two_grad, scaled_two, inverse_two, second_gain)
    second_gain_grad = jnp.sum(normed_two_grad * scaled_two, axis=(0, 1))
    second_bias_grad = jnp.sum(normed_two_grad, axis=(0, 1))
    down_bias_grad = jnp.sum(out_grad_values, axis=(0, 1))
    residual_grad = middle_grad.astype(jnp.bfloat16)
    out_bias_grad = jnp.sum(residual_grad.astype(jnp.float32), axis=(0, 1))
    branch_grad_all = lax.all_gather(residual_grad, "mp", axis=1, tiled=True)
    normed_part, coeffs_part, qkv_grad, qv_grad, memw_grad, memb_grad, outw_grad = attend_backward(
        branch_grad_all,
        normed_all,
        coeffs_all,
        flag_local,
        query_key_value_matrix,
        memory_weight,
        memory_bias,
        output_matrix,
        kept,
    )
    normed_one_grad, coeff_grad = (
        lax.psum_scatter(
            normed_part.astype(jnp.bfloat16), "mp", scatter_dimension=1, tiled=True
        ).astype(jnp.float32),
        lax.psum_scatter(
            coeffs_part.astype(jnp.bfloat16), "mp", scatter_dimension=1, tiled=True
        ).astype(jnp.float32),
    )
    input_grad = middle_grad + norm_back(normed_one_grad, scaled_one, inverse_one, first_gain)
    first_gain_grad = jnp.sum(normed_one_grad * scaled_one, axis=(0, 1))
    first_bias_grad = jnp.sum(normed_one_grad, axis=(0, 1))
    (
        qkv_grad,
        qv_grad,
        memw_grad,
        memb_grad,
        outw_grad,
        up_output_grad,
        upb_grad,
        down_output_grad,
    ) = lax.psum(
        (
            qkv_grad,
            qv_grad,
            memw_grad,
            memb_grad,
            outw_grad,
            up_output_grad,
            upb_grad,
            down_output_grad,
        ),
        "batch",
    )
    (
        first_gain_grad,
        first_bias_grad,
        out_bias_grad,
        second_gain_grad,
        second_bias_grad,
        down_bias_grad,
    ) = lax.psum(
        (
            first_gain_grad,
            first_bias_grad,
            out_bias_grad,
            second_gain_grad,
            second_bias_grad,
            down_bias_grad,
        ),
        ("batch", "mp"),
    )
    return (
        block_out,
        input_grad,
        coeff_grad,
        first_gain_grad,
        first_bias_grad,
        qkv_grad,
        qv_grad,
        memw_grad,
        memb_grad,
        outw_grad,
        out_bias_grad,
        second_gain_grad,
        second_bias_grad,
        up_output_grad,
        upb_grad,
        down_output_grad,
        down_bias_grad,
    )


def solution(mesh):
    placed = (
        P("batch", "mp", None),
        P("batch"),
        P("batch", "mp", None),
        P(),
        P(),
        P(None, None, "mp"),
        P(None, "mp"),
        P(None, "mp", None),
        P(None, "mp"),
        P("mp", None),
        P(),
        P(),
        P(),
        P(None, "mp"),
        P("mp"),
        P("mp", None),
        P(),
        P("batch", "mp", None),
    )
    return jax.shard_map(
        per_device,
        mesh=mesh,
        in_specs=placed,
        out_specs=(
            P("batch", "mp", None),
            P("batch", "mp", None),
            P("batch", "mp", None),
            P(),
            P(),
            P(None, None, "mp"),
            P(None, "mp"),
            P(None, "mp", None),
            P(None, "mp"),
            P("mp", None),
            P(),
            P(),
            P(),
            P(None, "mp"),
            P("mp"),
            P("mp", None),
            P(),
        ),
        check_vma=False,
    )
```

profile of v0, /device:TPU:0, one launch (start us, length us, event | category | flops | bytes accessed | tf_op | source)
XLA Modules:
  0.0 850.8 jit_solution(11959987445198987662)
XLA Ops:
  28.6 6.5 fusion.74
  41.1 4.6 fusion.29
  45.7 4.3 fusion.31
  50.0 7.1 fusion.54
  57.1 10.7 %fusion.34 = (f32[2,6,512]{2,1,0:T(8,128)S(1)}, f32[2,6,512,1024]{3,2,1,0:T(8,128)}) fusion(pred[512,1024]{1,0:T(8,128)(4,1)S(1)} %iota_compare_fusion, bf16[2,1024,6,64]{1,3,2,0:T(8,128)(2,1)S(1)} %bitcast.292, bf16[2,1024,6,64]{1,3,2,0:T(8,128)(2,1)S(1)} %add_convert_fusion.3), kind=kOutput, calls=%fused_computation.57 | convolution fusion | flops 824174592 | bytes 28073984 | tf_op jit(solution)/shard_map/sqhd,skhd->shqk/dot_general | solution.py:15
  68.1 7.7 fusion.24
  75.9 7.7 fusion.98
  85.9 7.3 fusion
  93.3 8.5 %fusion.102 = f32[2,512,6,64]{1,3,2,0:T(8,128)} fusion(bf16[2,1024,6,64]{1,3,2,0:T(8,128)(2,1)S(1)} %add_convert_fusion.4, f32[2,6,512]{2,1,0:T(8,128)S(1)} %fusion, f32[2,6,512]{2,1,0:T(8,128)S(1)} %get-tuple-element.164, f32[2,6,512,1024]{3,2,1,0:T(8,128)S(1)} %bitcast.288, pred[512,1024]{1,0:T(8,128)(4,1)S(1)} %iota_compare_fusion), kind=kOutput, calls=%fused_computation.147 | convolution fusion | flops 836763648 | bytes 28884992 | tf_op jit(solution)/shard_map/shqk,skhd->sqhd/dot_general | solution.py:15
  102.8 16.8 %fusion.70 = bf16[2,1024,6,64]{1,3,2,0:T(8,128)(2,1)S(1)} fusion(f32[2,512,6,64]{1,3,2,0:T(8,128)} %fusion.102, f32[2,512,6,64]{1,3,2,0:T(8,128)} %fusion.98, bf16[2,256,6,64]{1,3,2,0:T(8,128)(2,1)S(1)} %bitcast.314, f32[2,1024,6]{1,2,0:T(8,128)S(1)} %get-tuple-element.149, f32[2,1024,6]{1,2,0:T(8,128)S(1)} %get-tuple-element.151, ...), kind=kOutput, calls=%fused_computation.105 | convolution fusion | flops 427819008 | bytes 5260296 | tf_op jit(solution)/shard_map/slhn,snhd->slhd/dot_general | solution.py:15
  120.8 4.4 fusion.140
  125.3 15.8 %reduce-scatter.6.cloned.1.call-done = f32[2,512,768]{2,1,0:T(8,128)} async-done(((f32[2,1024,768]{2,1,0:T(8,128)}), f32[2,512,768]{2,1,0:T(8,128)}) %reduce-scatter.6.cloned.1.call-update) | async-done | bytes 3145744 | tf_op jit(solution)/shard_map/reduce_scatter | solution.py:277
  148.0 12.8 %all-gather.7.cloned.1.call-done = bf16[2,1024,768]{2,1,0:T(8,128)(2,1)} async-done(((bf16[2,512,768]{2,1,0:T(8,128)(2,1)}), bf16[2,1024,768]{2,1,0:T(8,128)(2,1)}) %all-gather.7.cloned.1.call-update) | async-done | bytes 3145744 | tf_op jit(solution)/shard_map/all_gather | solution.py:280
  160.8 13.4 %multiply_convert_fusion.2 = (bf16[2,1024,1536]{2,1,0:T(8,128)(2,1)}, f32[2,1024,1536]{2,1,0:T(8,128)}) fusion(f32[1536]{0:T(1024)S(1)} %convert_element_type.137, bf16[2,1024,768]{2,1,0:T(8,128)(2,1)} %all-gather.7.cloned.1.call-done, bf16[768,1536]{1,0:T(8,128)(2,1)S(1)} %copy-done), kind=kOutput, calls=%fused_computation.40 | convolution fusion | flops 4863295488 | bytes 24385536 | tf_op jit(solution)/shard_map/ahg,gm->ahm/dot_general | solution.py:15
  175.6 17.3 %convert_reduce_fusion = (f32[1536]{0:T(1024)}, bf16[2,1024,1536]{2,1,0:T(8,128)(2,1)S(1)}) fusion(f32[2,1024,1536]{2,1,0:T(8,128)} %get-tuple-element.171, f32[1536]{0:T(1024)S(1)} %convert_element_type.137, bf16[2,1024,768]{2,1,0:T(8,128)(2,1)} %all-gather.9.cloned.1.call-done, bf16[1536,768]{1,0:T(8,128)(2,1)} %param.47), kind=kOutput, calls=%fused_computation.34 | convolution fusion | flops 4904188416 | bytes 24391680 | tf_op jit(solution)/shard_map/kpo,wo->kpw/dot_general | solution.py:15
  195.6 6.9 fusion.82
  202.5 15.8 %reduce-scatter.10.cloned.1.call-done = f32[2,512,768]{2,1,0:T(8,128)} async-done(((f32[2,1024,768]{2,1,0:T(8,128)}), f32[2,512,768]{2,1,0:T(8,128)}) %reduce-scatter.10.cloned.1.call-update) | async-done | bytes 3145744 | tf_op jit(solution)/shard_map/reduce_scatter | solution.py:292
  218.3 4.7 multiply_reduce_fusion.2
  223.1 4.2 convert_reduce_fusion.5
  227.5 13.3 %all-gather.11.cloned.1.call-done = bf16[2,1024,768]{2,1,0:T(8,128)(2,1)} async-done(((bf16[2,512,768]{2,1,0:T(8,128)(2,1)}), bf16[2,1024,768]{2,1,0:T(8,128)(2,1)}) %all-gather.11.cloned.1.call-update) | async-done | bytes 3145744 | tf_op jit(solution)/shard_map/all_gather | solution.py:300
  240.8 3.4 convolution_convert_fusion
  244.3 8.0 fusion.99
  252.8 6.9 multiply_reduce_fusion.1
  259.6 7.1 multiply_convert_fusion.1
  266.8 3.2 multiply_bitcast_fusion.1
  272.4 4.1 fusion.112
  276.7 11.3 %fusion.6 = (f32[2,1024,6]{1,2,0:T(8,128)S(1)}, f32[2,1024,6]{1,2,0:T(8,128)S(1)}, f32[2,1024,6]{1,2,0:T(8,128)S(1)}) fusion(f32[2,1024,6]{1,2,0:T(8,128)S(1)} %copy-done.52, f32[2,1024,6]{1,2,0:T(8,128)S(1)} %copy-done.58, f32[256]{0:T(256)S(1)} %copy-done.90, f32[2,1024,6]{1,2,0:T(8,128)S(1)} %copy-done.54, f32[2,1024,6]{1,2,0:T(8,128)S(1)} %get-tuple-element.148, ...), kind=kOutput, calls=%fused_computation.17 | convolution fusion | flops 460025856 | bytes 2311172 | tf_op jit(solution)/shard_map/slhd,snhd->slhn/dot_general | solution.py:15
  288.3 5.3 fusion.109
  294.9 3.0 bitcast_convert_fusion.1
  298.0 18.1 %multiply_reduce_fusion = (f32[2,6,512]{2,1,0:T(8,128)S(1)}, f32[2,6,512,1024]{3,2,1,0:T(8,128)}) fusion(f32[2,6,512]{2,1,0:T(8,128)S(1)} %log_add_fusion, f32[2,6,512,1024]{3,2,1,0:T(8,128)} %get-tuple-element.165, pred[512,1024]{1,0:T(8,128)(4,1)S(1)} %copy-done.8, bf16[2,1024,6,64]{1,3,2,0:T(8,128)(2,1)} %copy-done.16, bf16[2,1024,6,64]{1,3,2,0:T(8,128)(2,1)} %bitcast.312), kind=kOutput, calls=%fused_computation.1 | convolution fusion | flops 836757504 | bytes 53264384 | tf_op jit(solution)/shard_map/sqhd,skhd->shqk/dot_general | solution.py:15
  316.1 13.5 %fusion.76 = bf16[2,1024,6,64]{1,3,2,0:T(8,128)(2,1)} fusion(f32[2,512,6,64]{1,3,2,0:T(8,128)} %fusion.99, f32[2,6,512]{2,1,0:T(8,128)S(1)} %log_add_fusion, f32[2,6,512,1024]{3,2,1,0:T(8,128)} %get-tuple-element.165, pred[512,1024]{1,0:T(8,128)(4,1)S(1)} %copy-done.8, bf16[2,1024,6,64]{1,3,2,0:T(8,128)(2,1)} %bitcast.313), kind=kOutput, calls=%fused_computation.113 | convolution fusion | flops 832045056 | bytes 29646848 | tf_op jit(solution)/shard_map/shqk,sqhd->skhd/dot_general | solution.py:15
  332.1 21.4 %multiply_convert_fusion = bf16[2,6,512,1024]{3,2,1,0:T(8,128)(2,1)} fusion(f32[2,6,512,1024]{3,2,1,0:T(8,128)} %get-tuple-element.169, f32[2,6,512]{2,1,0:T(8,128)S(1)} %get-tuple-element.168, f32[2,6,512]{2,1,0:T(8,128)S(1)} %log_add_fusion, f32[2,6,512,1024]{3,2,1,0:T(8,128)} %get-tuple-element.165, pred[512,1024]{1,0:T(8,128)(4,1)S(1)} %copy-done.8), kind=kLoop, calls=%fused_computation | loop fusion | flops 37748736 | bytes 63488000 | tf_op jit(solution)/shard_map/convert_element_type | solution.py:178
  353.5 8.6 %multiply_bitcast_fusion.2 = f32[2,512,6,64]{1,3,2,0:T(8,128)S(1)} fusion(bf16[2,1024,6,64]{1,3,2,0:T(8,128)(2,1)S(1)} %bitcast.294, bf16[2,6,512,1024]{3,2,1,0:T(8,128)(2,1)} %multiply_convert_fusion), kind=kOutput, calls=%fused_computation.143 | convolution fusion | flops 805699584 | bytes 15728640 | tf_op jit(solution)/shard_map/shqk,skhd->sqhd/dot_general | solution.py:15
  362.2 5.9 fusion.71
  370.6 8.4 fusion.77
  381.8 8.4 bitcast_convert_fusion
  390.3 9.0 %fusion.86 = bf16[2,1024,768]{2,1,0:T(8,128)(2,1)} fusion(bf16[2,1024,1536]{2,1,0:T(8,128)(2,1)} %get-tuple-element.170, bf16[1536,768]{1,0:T(8,128)(2,1)} %param.47), kind=kOutput, calls=%fused_computation.135 | convolution fusion | flops 4833411072 | bytes 11796480 | tf_op jit(solution)/shard_map/hom,mu->hou/dot_general | solution.py:15
  399.4 10.4 %convolution_bitcast_fusion.1 = f32[768,1536]{1,0:T(8,128)} fusion(bf16[2,1024,768]{2,1,0:T(8,128)(2,1)} %all-gather.7.cloned.1.call-done, bf16[2,1024,1536]{2,1,0:T(8,128)(2,1)} %copy-done.91), kind=kOutput, calls=%fused_computation.90 | convolution fusion | flops 4831838208 | bytes 14155776 | tf_op jit(solution)/shard_map/orx,ora->xa/dot_general | solution.py:15
  409.7 8.9 %convolution_bitcast_fusion = f32[1536,768]{1,0:T(8,128)} fusion(bf16[2,1024,1536]{2,1,0:T(8,128)(2,1)} %get-tuple-element.170, bf16[2,1024,768]{2,1,0:T(8,128)(2,1)S(1)} %copy-done.85), kind=kOutput, calls=%fused_computation.89 | convolution fusion | flops 4831838208 | bytes 14155776 | tf_op jit(solution)/shard_map/qro,qrv->ov/dot_general | solution.py:15
  418.6 6.1 fusion.89
  424.7 4.0 fusion.78
  432.0 13.3 %fusion.27 = f32[6,1,256,1]{2,1,3,0:T(1,128)S(1)} fusion(f32[2,1024,6,256]{1,3,2,0:T(8,128)} %copy-done.2, f32[6,2,1024,1]{2,0,1,3:T(8,128)S(1)} %bitcast.319), kind=kOutput, calls=%fused_computation.50 | convolution fusion | flops 37748736 | bytes 12638208 | tf_op jit(solution)/shard_map/transpose(jvp(slhn,hn->slh))/dot_general | solution.py:11
  445.4 13.4 %fusion.25 = f32[6,1,256,1]{2,1,3,0:T(1,128)S(1)} fusion(f32[2,1024,6,256]{1,3,2,0:T(8,128)} %copy-done.2, f32[6,2,1024,1]{2,0,1,3:T(8,128)S(1)} %bitcast.318), kind=kOutput, calls=%fused_computation.48 | convolution fusion | flops 37748736 | bytes 12638208 | tf_op jit(solution)/shard_map/transpose(jvp(slhn,hn->slh))/dot_general | solution.py:11
  460.5 81.6 %all-reduce.7 = (f32[2,384]{1,0:T(2,128)}, f32[2,6,256]{2,1,0:T(8,128)S(1)}, f32[2,6]{1,0:T(2,128)}, f32[1536]{0:T(1024)}) all-reduce(f32[2,384]{1,0:T(2,128)S(1)} %convert_reduce_fusion.1, f32[2,6,256]{2,1,0:T(8,128)S(1)} %pad_add_fusion, f32[2,6]{1,0:T(2,128)S(1)} %pad_add_fusion.1, ...), channel_id=1, replica_groups=mesh['batch'=16,'mp'=2] {'batch'}, use_global_device_ids=true, to_apply=%region_28.29 | all-reduce | flops 5388 | bytes 43104 | tf_op jit(solution)/shard_map/psum | solution.py:332
  547.7 8.3 fusion.66
  556.0 40.4 %all-reduce.6 = (f32[768]{0:T(1024)}, f32[768]{0:T(1024)}, f32[768]{0:T(1024)}, f32[768]{0:T(1024)}, f32[768]{0:T(1024)}, /*index=5*/f32[768]{0:T(1024)}) all-reduce(f32[768]{0:T(1024)S(1)} %get-tuple-element.115, f32[768]{0:T(1024)S(1)} %get-tuple-element.120, ...), channel_id=1, replica_groups=mesh['batch'=16,'mp'=2] {'batch','mp'}, use_global_device_ids=true, to_apply=%region_23.24 | all-reduce | flops 4608 | bytes 36864 | tf_op jit(solution)/shard_map/psum | solution.py:352
  596.4 236.2 %all-reduce.11.cloned.1.call-done = (f32[768,3,384]{2,0,1:T(8,128)}, f32[384,768]{1,0:T(8,128)}, f32[768,1536]{1,0:T(8,128)}, f32[1536,768]{1,0:T(8,128)}) async-done(((f32[768,3,384]{2,0,1:T(8,128)}, f32[384,768]{1,0:T(8,128)}, f32[768,1536]{1,0:T(8,128)}, f32[1536,768]{1,0:T(8,128)}), (f32[768,3,384]{2,0,1:T(8,128)}, f32[384,768]{1,0:T(8,128)}, f32[768,1536]{1,0:T(8,128)}, ...) | async-done | bytes 14155792 | tf_op jit(solution)/shard_map/psum | solution.py:332
  832.7 4.2 copy.187
  (303 shorter events, 72.5 us)
Async XLA Ops:
  7.2 153.6 %copy-start = (bf16[768,1536]{1,0:T(8,128)(2,1)S(1)}, bf16[768,1536]{1,0:T(8,128)(2,1)}, u32[]{:S(2)}) copy-start(bf16[768,1536]{1,0:T(8,128)(2,1)} %param.45) | copy-start | bytes 7077892
  7.2 21.4 %all-gather.5.cloned.1.call-start = ((), (), s32[]{:S(2)}) async-start(), calls=%async_computation.5 | async-start | bytes 4718592 | tf_op jit(solution)/shard_map/all_gather | solution.py:264
  13.7 127.4 %reduce-scatter.6.cloned.1.call-start = ((), (), s32[]{:S(2)}) async-start(), calls=%async_computation.6 | async-start | bytes 9437184 | tf_op jit(solution)/shard_map/reduce_scatter | solution.py:277
  20.1 19.1 %copy-start.30 = (bf16[2,256,1,384]{1,3,0,2:T(8,128)(2,1)}, bf16[2,256,1,384]{1,3,0,2:T(8,128)(2,1)S(1)}, u32[]{:S(2)}) copy-start(bf16[2,256,1,384]{1,3,0,2:T(8,128)(2,1)S(1)} %copy.61) | copy-start | bytes 1179652
  21.7 54.1 %copy-start.18 = (pred[512,512]{0,1:T(8,128)(4,1)}, pred[512,512]{0,1:T(8,128)(4,1)S(1)}, u32[]{:S(2)}) copy-start(pred[512,512]{0,1:T(8,128)(4,1)S(1)} %iota_compare_fusion.1) | copy-start | bytes 786436
  25.9 67.4 %copy-start.7 = (pred[512,1024]{1,0:T(8,128)(4,1)}, pred[512,1024]{1,0:T(8,128)(4,1)S(1)}, u32[]{:S(2)}) copy-start(pred[512,1024]{1,0:T(8,128)(4,1)S(1)} %iota_compare_fusion) | copy-start | bytes 1572868
  39.3 17.9 %copy-start.9 = (bf16[2,1024,6,64]{1,3,2,0:T(8,128)(2,1)}, bf16[2,1024,6,64]{1,3,2,0:T(8,128)(2,1)S(1)}, u32[]{:S(2)}) copy-start(bf16[2,1024,6,64]{1,3,2,0:T(8,128)(2,1)S(1)} %add_convert_fusion.3) | copy-start | bytes 4718596
  45.7 56.3 %copy-start.34 = (f32[6,1,2,1024]{3,1,2,0:T(1,128)}, f32[6,1,2,1024]{3,1,2,0:T(1,128)S(1)}, u32[]{:S(2)}) copy-start(f32[6,1,2,1024]{3,1,2,0:T(1,128)S(1)} %fusion.29) | copy-start | bytes 147460
  50.0 51.9 %copy-start.36 = (f32[6,1,2,1024]{3,1,2,0:T(1,128)}, f32[6,1,2,1024]{3,1,2,0:T(1,128)S(1)}, u32[]{:S(2)}) copy-start(f32[6,1,2,1024]{3,1,2,0:T(1,128)S(1)} %fusion.31) | copy-start | bytes 147460
  68.1 25.2 %copy-start.16 = (bf16[2,1024,6,64]{1,3,2,0:T(8,128)(2,1)}, bf16[2,1024,6,64]{1,3,2,0:T(8,128)(2,1)S(1)}, u32[]{:S(2)}) copy-start(bf16[2,1024,6,64]{1,3,2,0:T(8,128)(2,1)S(1)} %add_convert_fusion.4) | copy-start | bytes 4718596
  68.1 15.5 %slice-start = ((s8[25165824]{0:T(1024)(128)(4,1)}), s8[4194304]{0:T(1024)(128)(4,1)S(1)}, s32[]{:S(2)}) async-start(s8[25165824]{0:T(1024)(128)(4,1)} %bitcast.287), calls=%async_computation.15 | async-start | bytes 8388608
  68.1 15.5 %slice-start.1 = ((s8[25165824]{0:T(1024)(128)(4,1)}), s8[4194304]{0:T(1024)(128)(4,1)S(1)}, s32[]{:S(2)}) async-start(s8[25165824]{0:T(1024)(128)(4,1)} %bitcast.287), calls=%async_computation.16 | async-start | bytes 8388608
  102.0 17.6 %copy-start.57 = (f32[2,1024,6]{1,2,0:T(8,128)}, f32[2,1024,6]{1,2,0:T(8,128)S(1)}, u32[]{:S(2)}) copy-start(f32[2,1024,6]{1,2,0:T(8,128)S(1)} %fusion.189) | copy-start | bytes 147460
  102.8 16.8 %copy-start.53 = (f32[2,1024,6]{1,2,0:T(8,128)}, f32[2,1024,6]{1,2,0:T(8,128)S(1)}, u32[]{:S(2)}) copy-start(f32[2,1024,6]{1,2,0:T(8,128)S(1)} %get-tuple-element.151) | copy-start | bytes 147460
  102.8 16.8 %copy-start.55 = (f32[2,1024,6]{1,2,0:T(8,128)}, f32[2,1024,6]{1,2,0:T(8,128)S(1)}, u32[]{:S(2)}) copy-start(f32[2,1024,6]{1,2,0:T(8,128)S(1)} %get-tuple-element.149) | copy-start | bytes 147460
  102.8 18.0 %copy-start.38 = (bf16[384,768]{1,0:T(8,128)(2,1)S(1)}, bf16[384,768]{1,0:T(8,128)(2,1)}, u32[]{:S(2)}) copy-start(bf16[384,768]{1,0:T(8,128)(2,1)} %param.41) | copy-start | bytes 1769476
  125.2 15.9 %copy-start.79 = (f32[768]{0:T(1024)S(1)}, f32[768]{0:T(1024)}, u32[]{:S(2)}) copy-start(f32[768]{0:T(1024)} %param.42) | copy-start | bytes 9220
  125.2 35.6 %all-gather.7.cloned.1.call-start = ((), (), s32[]{:S(2)}) async-start(), calls=%async_computation.7 | async-start | bytes 4718592 | tf_op jit(solution)/shard_map/all_gather | solution.py:280
  144.0 79.1 %copy-start.44 = (f32[2,512]{1,0:T(2,128)}, f32[2,512]{1,0:T(2,128)S(1)}, u32[]{:S(2)}) copy-start(f32[2,512]{1,0:T(2,128)S(1)} %broadcast_multiply_fusion.6) | copy-start | bytes 12292
  145.6 77.4 %copy-start.48 = (f32[2,512]{1,0:T(2,128)}, f32[2,512]{1,0:T(2,128)S(1)}, u32[]{:S(2)}) copy-start(f32[2,512]{1,0:T(2,128)S(1)} %add_rsqrt_fusion) | copy-start | bytes 12292
  147.3 28.2 %all-gather.9.cloned.1.call-start = ((), (), s32[]{:S(2)}) async-start(), calls=%async_computation.9 | async-start | bytes 4718592 | tf_op jit(solution)/shard_map/all_gather | solution.py:288
  147.9 70.4 %reduce-scatter.10.cloned.1.call-start = ((), (), s32[]{:S(2)}) async-start(), calls=%async_computation.10 | async-start | bytes 9437184 | tf_op jit(solution)/shard_map/reduce_scatter | solution.py:292
  202.5 20.6 %copy-start.14 = (bf16[2,512,768]{2,1,0:T(8,128)(2,1)S(1)}, bf16[2,512,768]{2,1,0:T(8,128)(2,1)}, u32[]{:S(2)}) copy-start(bf16[2,512,768]{2,1,0:T(8,128)(2,1)} %param.49) | copy-start | bytes 4718596
  202.5 38.3 %all-gather.11.cloned.1.call-start = ((), (), s32[]{:S(2)}) async-start(), calls=%async_computation.11 | async-start | bytes 4718592 | tf_op jit(solution)/shard_map/all_gather | solution.py:300
  227.4 315.4 %reduce-scatter.14.cloned.1.call-start = ((), (), s32[]{:S(2)}) async-start(), calls=%async_computation.13 | async-start | bytes 1179648 | tf_op jit(solution)/shard_map/reduce_scatter | solution.py:316
  227.5 16.8 %copy-start.19 = (pred[512,512]{0,1:T(8,128)(4,1)S(1)}, pred[512,512]{0,1:T(8,128)(4,1)}, u32[]{:S(2)}) copy-start(pred[512,512]{0,1:T(8,128)(4,1)} %copy-done.18) | copy-start | bytes 786436
  240.8 11.5 %slice-start.6 = ((s8[12582912]{0:T(1024)(128)(4,1)}), s8[4194304]{0:T(1024)(128)(4,1)S(1)}, s32[]{:S(2)}) async-start(s8[12582912]{0:T(1024)(128)(4,1)} %bitcast.289), calls=%async_computation.21 | async-start | bytes 8388608
  244.3 28.1 %copy-start.32 = (bf16[2,1024,384]{1,2,0:T(8,128)(2,1)}, bf16[2,1024,384]{1,2,0:T(8,128)(2,1)S(1)}, u32[]{:S(2)}) copy-start(bf16[2,1024,384]{1,2,0:T(8,128)(2,1)S(1)} %convolution_convert_fusion) | copy-start | bytes 4718596
  276.7 11.4 %copy-start.35 = (f32[6,1,2,1024]{3,1,2,0:T(1,128)S(1)}, f32[6,1,2,1024]{3,1,2,0:T(1,128)}, u32[]{:S(2)}) copy-start(f32[6,1,2,1024]{3,1,2,0:T(1,128)} %copy-done.34) | copy-start | bytes 147460
  276.7 11.6 %copy-start.76 = (f32[6,256]{1,0:T(8,128)S(1)}, f32[6,256]{1,0:T(8,128)}, u32[]{:S(2)}) copy-start(f32[6,256]{1,0:T(8,128)} %get-tuple-element.154) | copy-start | bytes 18436
  276.7 11.6 %copy-start.77 = (f32[6,256]{1,0:T(8,128)S(1)}, f32[6,256]{1,0:T(8,128)}, u32[]{:S(2)}) copy-start(f32[6,256]{1,0:T(8,128)} %get-tuple-element.152) | copy-start | bytes 18436
  288.3 73.9 %copy-start.42 = (f32[6,2,1024]{2,0,1:T(8,128)}, f32[6,2,1024]{2,0,1:T(8,128)S(1)}, u32[]{:S(2)}) copy-start(f32[6,2,1024]{2,0,1:T(8,128)S(1)} %get-tuple-element.174) | copy-start | bytes 147460
  297.9 246.8 %reduce-scatter.12.cloned.1.call-start = ((), (), s32[]{:S(2)}) async-start(), calls=%async_computation.12 | async-start | bytes 4718592 | tf_op jit(solution)/shard_map/reduce_scatter | solution.py:313
  332.1 21.4 %copy-start.13 = (bf16[2,1024,1,384]{1,3,2,0:T(8,128)(2,1)S(1)}, bf16[2,1024,1,384]{1,3,2,0:T(8,128)(2,1)}, u32[]{:S(2)}) copy-start(bf16[2,1024,1,384]{1,3,2,0:T(8,128)(2,1)} %slice.267) | copy-start | bytes 4718596
  390.2 157.4 %reduce-scatter.8.cloned.1.call-start = ((), (), s32[]{:S(2)}) async-start(), calls=%async_computation.8 | async-start | bytes 4718592 | tf_op jit(solution)/shard_map/reduce_scatter | solution.py:284
  399.3 433.3 %all-reduce.11.cloned.1.call-start = ((), (), s32[]{:S(2)}) async-start(), calls=%async_computation.14 | async-start | bytes 28311552 | tf_op jit(solution)/shard_map/psum | solution.py:332
  445.4 13.7 %copy-start.22 = (bf16[2,1024,1,384]{3,1,2,0:T(8,128)(2,1)S(1)}, bf16[2,1024,1,384]{3,1,2,0:T(8,128)(2,1)}, u32[]{:S(2)}) copy-start(bf16[2,1024,1,384]{3,1,2,0:T(8,128)(2,1)} %copy.69) | copy-start | bytes 4718596
  445.4 13.7 %copy-start.24 = (bf16[2,1024,1,384]{3,1,2,0:T(8,128)(2,1)S(1)}, bf16[2,1024,1,384]{3,1,2,0:T(8,128)(2,1)}, u32[]{:S(2)}) copy-start(bf16[2,1024,1,384]{3,1,2,0:T(8,128)(2,1)} %copy.70) | copy-start | bytes 4718596
  459.8 84.9 %copy-start.5 = (bf16[2,512,768]{2,1,0:T(8,128)(2,1)S(1)}, bf16[2,512,768]{2,1,0:T(8,128)(2,1)}, u32[]{:S(2)}) copy-start(bf16[2,512,768]{2,1,0:T(8,128)(2,1)} %param.32) | copy-start | bytes 4718596
  459.8 84.9 %copy-start.47 = (f32[2,512]{1,0:T(2,128)S(1)}, f32[2,512]{1,0:T(2,128)}, u32[]{:S(2)}) copy-start(f32[2,512]{1,0:T(2,128)} %copy-done.46) | copy-start | bytes 12292
  459.8 84.9 %copy-start.51 = (f32[2,512]{1,0:T(2,128)S(1)}, f32[2,512]{1,0:T(2,128)}, u32[]{:S(2)}) copy-start(f32[2,512]{1,0:T(2,128)} %copy-done.50) | copy-start | bytes 12292
  459.9 84.9 %copy-start.62 = (f32[768]{0:T(1024)S(1)}, f32[768]{0:T(1024)}, u32[]{:S(2)}) copy-start(f32[768]{0:T(1024)} %param.35) | copy-start | bytes 9220
  459.9 87.7 %copy-start.45 = (f32[2,512]{1,0:T(2,128)S(1)}, f32[2,512]{1,0:T(2,128)}, u32[]{:S(2)}) copy-start(f32[2,512]{1,0:T(2,128)} %copy-done.44) | copy-start | bytes 12292
  459.9 87.7 %copy-start.49 = (f32[2,512]{1,0:T(2,128)S(1)}, f32[2,512]{1,0:T(2,128)}, u32[]{:S(2)}) copy-start(f32[2,512]{1,0:T(2,128)} %copy-done.48) | copy-start | bytes 12292
  459.9 87.7 %copy-start.60 = (f32[768]{0:T(1024)S(1)}, f32[768]{0:T(1024)}, u32[]{:S(2)}) copy-start(f32[768]{0:T(1024)} %param.43) | copy-start | bytes 9220
  459.9 87.7 %copy-start.64 = (f32[2,512]{1,0:T(2,128)S(1)}, f32[2,512]{1,0:T(2,128)}, u32[]{:S(2)}) copy-start(f32[2,512]{1,0:T(2,128)} %copy-done.63) | copy-start | bytes 12292
  459.9 87.7 %copy-start.66 = (f32[2,512]{1,0:T(2,128)S(1)}, f32[2,512]{1,0:T(2,128)}, u32[]{:S(2)}) copy-start(f32[2,512]{1,0:T(2,128)} %copy-done.65) | copy-start | bytes 12292
  459.9 87.7 %copy-start.81 = (f32[768]{0:T(1024)S(1)}, f32[768]{0:T(1024)}, u32[]{:S(2)}) copy-start(f32[768]{0:T(1024)} %param.48) | copy-start | bytes 9220
  (67 other events, 383.2 us)
Sparse Core Ops, SparseCore 0:
  13.8 14.8 all-gather.4
  125.3 15.6 reduce-scatter.5
  147.5 13.2 all-gather.6
  162.3 13.2 all-gather.8
  202.6 15.6 reduce-scatter.9
  227.5 13.2 all-gather.10
  298.0 9.4 reduce-scatter.13
  390.3 12.0 reduce-scatter.11
  404.7 12.0 reduce-scatter.7
  431.3 401.2 all-reduce.10
where the time goes:
time: 861 us; the launch traced here: 851 us
  waiting for transfers between devices  299 us (35%)
  matrix products  290 us (34%)
  blocking collectives  125 us (15%)
  other arithmetic  83.4 us (10%)
  local copies, waits for them, and re-layouts  37.8 us (4%)
  between operations  15.9 us (2%)
    dot_general x33, matrix products, matrix_multiply(): jnp.einsum(form, left_side, right_side, preferred_element_type=jnp.float32)  254 us
    psum x1, waiting for transfers between devices, per_device(): lax.psum((qkv_grad, qv_grad, memw_grad, memb_grad, outw_grad, up_output_g...  236 us
    psum x1, blocking collectives, per_device(): lax.psum((qkv_grad, qv_grad, memw_grad, memb_grad, outw_grad, up_output_g...  81.6 us
    psum x1, blocking collectives, per_device(): lax.psum((first_gain_grad, first_bias_grad, out_bias_grad, second_gain_gr...  40.4 us
    dot_general x4, matrix products, product(): jnp.einsum(form, left_side, right_side, precision=lax.Precision.HIGHEST)  35.6 us
    convert_element_type x2, other arithmetic, attend_backward(): (weights * (weights_grad - inner_sum)).astype(jnp.bfloat16)  28.5 us
    unnamed x215, local copies, waits for them, and re-layouts  21.9 us
  transfers between devices with their start and end apart: 10, of which 7 were waited for; matrix products, arithmetic and copies ran while one was open for 23% of the time, Pallas kernels for 0%

commit v1 on v0

--- a/solution.py
+++ b/solution.py
@@ -350,15 +350,18 @@
         second_bias_grad,
         down_bias_grad,
     ) = lax.psum(
-        (
-            first_gain_grad,
-            first_bias_grad,
-            out_bias_grad,
-            second_gain_grad,
-            second_bias_grad,
-            down_bias_grad,
+        lax.psum(
+            (
+                first_gain_grad,
+                first_bias_grad,
+                out_bias_grad,
+                second_gain_grad,
+                second_bias_grad,
+                down_bias_grad,
+            ),
+            "batch",
         ),
-        ("batch", "mp"),
+        "mp",
     )
     return (
         block_out,

time: 861 us -> 859 us (level)
  blocking collectives: 125 us -> 88.9 us
  waiting for transfers between devices: 299 us -> 333 us
    psum x1, blocking collectives: 81.6 us -> 4 us  [per_device(): lax.psum(lax.psum((first_gain_grad, first_bias_grad, out_bias_grad, secon...]
    psum x1, blocking collectives: 40.4 us -> 82.5 us  [per_device(): lax.psum((first_gain_grad, first_bias_grad, out_bias_grad, second_gain_gr...]
    psum x1, waiting for transfers between devices: 236 us -> 270 us  [per_device(): lax.psum((qkv_grad, qv_grad, memw_grad, memb_grad, outw_grad, up_output_g...]
where the time goes in v1:
time: 859 us; the launch traced here: 849 us
  waiting for transfers between devices  333 us (39%)
  matrix products  290 us (34%)
  blocking collectives  88.9 us (10%)
  other arithmetic  83.3 us (10%)
  local copies, waits for them, and re-layouts  37.7 us (4%)
  between operations  15.8 us (2%)
    psum x1, waiting for transfers between devices, per_device(): lax.psum((qkv_grad, qv_grad, memw_grad, memb_grad, outw_grad, up_output_g...  270 us
    dot_general x33, matrix products, matrix_multiply(): jnp.einsum(form, left_side, right_side, preferred_element_type=jnp.float32)  254 us
    psum x1, blocking collectives, per_device(): lax.psum((first_gain_grad, first_bias_grad, out_bias_grad, second_gain_gr...  82.5 us
    dot_general x4, matrix products, product(): jnp.einsum(form, left_side, right_side, precision=lax.Precision.HIGHEST)  35.6 us
    convert_element_type x2, other arithmetic, attend_backward(): (weights * (weights_grad - inner_sum)).astype(jnp.bfloat16)  28.5 us
    unnamed x215, local copies, waits for them, and re-layouts  21.8 us
  transfers between devices with their start and end apart: 10, of which 7 were waited for; matrix products, arithmetic and copies ran while one was open for 23% of the time, Pallas kernels for 0%

profile of v1, /device:TPU:0, one launch (start us, length us, event | category | flops | bytes accessed | tf_op | source)
XLA Modules:
  0.0 849.1 jit_solution(3796491954438523466)
XLA Ops:
  28.6 6.5 fusion.74
  41.1 4.6 fusion.29
  45.7 4.3 fusion.31
  50.0 7.1 fusion.54
  57.1 10.7 %fusion.34 = (f32[2,6,512]{2,1,0:T(8,128)S(1)}, f32[2,6,512,1024]{3,2,1,0:T(8,128)}) fusion(pred[512,1024]{1,0:T(8,128)(4,1)S(1)} %iota_compare_fusion, bf16[2,1024,6,64]{1,3,2,0:T(8,128)(2,1)S(1)} %bitcast.292, bf16[2,1024,6,64]{1,3,2,0:T(8,128)(2,1)S(1)} %add_convert_fusion.3), kind=kOutput, calls=%fused_computation.57 | convolution fusion | flops 824174592 | bytes 28073984 | tf_op jit(solution)/shard_map/sqhd,skhd->shqk/dot_general | solution.py:15
  68.1 7.7 fusion.24
  75.9 7.7 fusion.98
  85.9 7.3 fusion
  93.3 8.5 %fusion.102 = f32[2,512,6,64]{1,3,2,0:T(8,128)} fusion(bf16[2,1024,6,64]{1,3,2,0:T(8,128)(2,1)S(1)} %add_convert_fusion.4, f32[2,6,512]{2,1,0:T(8,128)S(1)} %fusion, f32[2,6,512]{2,1,0:T(8,128)S(1)} %get-tuple-element.170, f32[2,6,512,1024]{3,2,1,0:T(8,128)S(1)} %bitcast.288, pred[512,1024]{1,0:T(8,128)(4,1)S(1)} %iota_compare_fusion), kind=kOutput, calls=%fused_computation.147 | convolution fusion | flops 836763648 | bytes 28884992 | tf_op jit(solution)/shard_map/shqk,skhd->sqhd/dot_general | solution.py:15
  102.8 16.8 %fusion.70 = bf16[2,1024,6,64]{1,3,2,0:T(8,128)(2,1)S(1)} fusion(f32[2,512,6,64]{1,3,2,0:T(8,128)} %fusion.102, f32[2,512,6,64]{1,3,2,0:T(8,128)} %fusion.98, bf16[2,256,6,64]{1,3,2,0:T(8,128)(2,1)S(1)} %bitcast.314, f32[2,1024,6]{1,2,0:T(8,128)S(1)} %get-tuple-element.155, f32[2,1024,6]{1,2,0:T(8,128)S(1)} %get-tuple-element.157, ...), kind=kOutput, calls=%fused_computation.105 | convolution fusion | flops 427819008 | bytes 5260296 | tf_op jit(solution)/shard_map/slhn,snhd->slhd/dot_general | solution.py:15
  120.8 4.4 fusion.140
  125.3 15.8 %reduce-scatter.6.cloned.1.call-done = f32[2,512,768]{2,1,0:T(8,128)} async-done(((f32[2,1024,768]{2,1,0:T(8,128)}), f32[2,512,768]{2,1,0:T(8,128)}) %reduce-scatter.6.cloned.1.call-update) | async-done | bytes 3145744 | tf_op jit(solution)/shard_map/reduce_scatter | solution.py:277
  148.0 12.8 %all-gather.7.cloned.1.call-done = bf16[2,1024,768]{2,1,0:T(8,128)(2,1)} async-done(((bf16[2,512,768]{2,1,0:T(8,128)(2,1)}), bf16[2,1024,768]{2,1,0:T(8,128)(2,1)}) %all-gather.7.cloned.1.call-update) | async-done | bytes 3145744 | tf_op jit(solution)/shard_map/all_gather | solution.py:280
  160.8 13.4 %multiply_convert_fusion.2 = (bf16[2,1024,1536]{2,1,0:T(8,128)(2,1)}, f32[2,1024,1536]{2,1,0:T(8,128)}) fusion(f32[1536]{0:T(1024)S(1)} %convert_element_type.137, bf16[2,1024,768]{2,1,0:T(8,128)(2,1)} %all-gather.7.cloned.1.call-done, bf16[768,1536]{1,0:T(8,128)(2,1)S(1)} %copy-done), kind=kOutput, calls=%fused_computation.40 | convolution fusion | flops 4863295488 | bytes 24385536 | tf_op jit(solution)/shard_map/ahg,gm->ahm/dot_general | solution.py:15
  175.6 17.3 %convert_reduce_fusion = (f32[1536]{0:T(1024)}, bf16[2,1024,1536]{2,1,0:T(8,128)(2,1)S(1)}) fusion(f32[2,1024,1536]{2,1,0:T(8,128)} %get-tuple-element.177, f32[1536]{0:T(1024)S(1)} %convert_element_type.137, bf16[2,1024,768]{2,1,0:T(8,128)(2,1)} %all-gather.9.cloned.1.call-done, bf16[1536,768]{1,0:T(8,128)(2,1)} %param.47), kind=kOutput, calls=%fused_computation.34 | convolution fusion | flops 4904188416 | bytes 24391680 | tf_op jit(solution)/shard_map/kpo,wo->kpw/dot_general | solution.py:15
  195.6 6.9 fusion.82
  202.5 15.8 %reduce-scatter.10.cloned.1.call-done = f32[2,512,768]{2,1,0:T(8,128)} async-done(((f32[2,1024,768]{2,1,0:T(8,128)}), f32[2,512,768]{2,1,0:T(8,128)}) %reduce-scatter.10.cloned.1.call-update) | async-done | bytes 3145744 | tf_op jit(solution)/shard_map/reduce_scatter | solution.py:292
  218.3 4.7 multiply_reduce_fusion.2
  223.1 4.2 convert_reduce_fusion.5
  227.5 13.3 %all-gather.11.cloned.1.call-done = bf16[2,1024,768]{2,1,0:T(8,128)(2,1)} async-done(((bf16[2,512,768]{2,1,0:T(8,128)(2,1)}), bf16[2,1024,768]{2,1,0:T(8,128)(2,1)}) %all-gather.11.cloned.1.call-update) | async-done | bytes 3145744 | tf_op jit(solution)/shard_map/all_gather | solution.py:300
  240.8 3.4 convolution_convert_fusion
  244.3 8.0 fusion.99
  252.8 6.9 multiply_reduce_fusion.1
  259.6 7.1 multiply_convert_fusion.1
  266.8 3.2 multiply_bitcast_fusion.1
  272.4 4.1 fusion.112
  276.7 11.3 %fusion.6 = (f32[2,1024,6]{1,2,0:T(8,128)S(1)}, f32[2,1024,6]{1,2,0:T(8,128)S(1)}, f32[2,1024,6]{1,2,0:T(8,128)S(1)}) fusion(f32[2,1024,6]{1,2,0:T(8,128)S(1)} %copy-done.52, f32[2,1024,6]{1,2,0:T(8,128)S(1)} %copy-done.58, f32[256]{0:T(256)S(1)} %copy-done.90, f32[2,1024,6]{1,2,0:T(8,128)S(1)} %copy-done.54, f32[2,1024,6]{1,2,0:T(8,128)S(1)} %get-tuple-element.154, ...), kind=kOutput, calls=%fused_computation.17 | convolution fusion | flops 460025856 | bytes 2311172 | tf_op jit(solution)/shard_map/slhd,snhd->slhn/dot_general | solution.py:15
  288.3 5.3 fusion.109
  294.9 3.0 bitcast_convert_fusion.1
  298.0 18.1 %multiply_reduce_fusion = (f32[2,6,512]{2,1,0:T(8,128)S(1)}, f32[2,6,512,1024]{3,2,1,0:T(8,128)}) fusion(f32[2,6,512]{2,1,0:T(8,128)S(1)} %log_add_fusion, f32[2,6,512,1024]{3,2,1,0:T(8,128)} %get-tuple-element.171, pred[512,1024]{1,0:T(8,128)(4,1)S(1)} %copy-done.8, bf16[2,1024,6,64]{1,3,2,0:T(8,128)(2,1)} %copy-done.16, bf16[2,1024,6,64]{1,3,2,0:T(8,128)(2,1)} %bitcast.312), kind=kOutput, calls=%fused_computation.1 | convolution fusion | flops 836757504 | bytes 53264384 | tf_op jit(solution)/shard_map/sqhd,skhd->shqk/dot_general | solution.py:15
  316.1 13.5 %fusion.76 = bf16[2,1024,6,64]{1,3,2,0:T(8,128)(2,1)} fusion(f32[2,512,6,64]{1,3,2,0:T(8,128)} %fusion.99, f32[2,6,512]{2,1,0:T(8,128)S(1)} %log_add_fusion, f32[2,6,512,1024]{3,2,1,0:T(8,128)} %get-tuple-element.171, pred[512,1024]{1,0:T(8,128)(4,1)S(1)} %copy-done.8, bf16[2,1024,6,64]{1,3,2,0:T(8,128)(2,1)} %bitcast.313), kind=kOutput, calls=%fused_computation.113 | convolution fusion | flops 832045056 | bytes 29646848 | tf_op jit(solution)/shard_map/shqk,sqhd->skhd/dot_general | solution.py:15
  332.1 21.4 %multiply_convert_fusion = bf16[2,6,512,1024]{3,2,1,0:T(8,128)(2,1)} fusion(f32[2,6,512,1024]{3,2,1,0:T(8,128)} %get-tuple-element.175, f32[2,6,512]{2,1,0:T(8,128)S(1)} %get-tuple-element.174, f32[2,6,512]{2,1,0:T(8,128)S(1)} %log_add_fusion, f32[2,6,512,1024]{3,2,1,0:T(8,128)} %get-tuple-element.171, pred[512,1024]{1,0:T(8,128)(4,1)S(1)} %copy-done.8), kind=kLoop, calls=%fused_computation | loop fusion | flops 37748736 | bytes 63488000 | tf_op jit(solution)/shard_map/convert_element_type | solution.py:178
  353.5 8.6 %multiply_bitcast_fusion.2 = f32[2,512,6,64]{1,3,2,0:T(8,128)S(1)} fusion(bf16[2,1024,6,64]{1,3,2,0:T(8,128)(2,1)S(1)} %bitcast.294, bf16[2,6,512,1024]{3,2,1,0:T(8,128)(2,1)} %multiply_convert_fusion), kind=kOutput, calls=%fused_computation.143 | convolution fusion | flops 805699584 | bytes 15728640 | tf_op jit(solution)/shard_map/shqk,skhd->sqhd/dot_general | solution.py:15
  362.2 5.9 fusion.71
  370.6 8.4 fusion.77
  381.8 8.4 bitcast_convert_fusion
  390.3 9.0 %fusion.86 = bf16[2,1024,768]{2,1,0:T(8,128)(2,1)} fusion(bf16[2,1024,1536]{2,1,0:T(8,128)(2,1)} %get-tuple-element.176, bf16[1536,768]{1,0:T(8,128)(2,1)} %param.47), kind=kOutput, calls=%fused_computation.135 | convolution fusion | flops 4833411072 | bytes 11796480 | tf_op jit(solution)/shard_map/hom,mu->hou/dot_general | solution.py:15
  399.4 10.4 %convolution_bitcast_fusion.1 = f32[768,1536]{1,0:T(8,128)} fusion(bf16[2,1024,768]{2,1,0:T(8,128)(2,1)} %all-gather.7.cloned.1.call-done, bf16[2,1024,1536]{2,1,0:T(8,128)(2,1)} %copy-done.91), kind=kOutput, calls=%fused_computation.90 | convolution fusion | flops 4831838208 | bytes 14155776 | tf_op jit(solution)/shard_map/orx,ora->xa/dot_general | solution.py:15
  409.7 8.9 %convolution_bitcast_fusion = f32[1536,768]{1,0:T(8,128)} fusion(bf16[2,1024,1536]{2,1,0:T(8,128)(2,1)} %get-tuple-element.176, bf16[2,1024,768]{2,1,0:T(8,128)(2,1)S(1)} %copy-done.85), kind=kOutput, calls=%fused_computation.89 | convolution fusion | flops 4831838208 | bytes 14155776 | tf_op jit(solution)/shard_map/qro,qrv->ov/dot_general | solution.py:15
  418.6 6.1 fusion.89
  424.7 4.0 fusion.78
  432.0 13.3 %fusion.27 = f32[6,1,256,1]{2,1,3,0:T(1,128)S(1)} fusion(f32[2,1024,6,256]{1,3,2,0:T(8,128)} %copy-done.2, f32[6,2,1024,1]{2,0,1,3:T(8,128)S(1)} %bitcast.319), kind=kOutput, calls=%fused_computation.50 | convolution fusion | flops 37748736 | bytes 12638208 | tf_op jit(solution)/shard_map/transpose(jvp(slhn,hn->slh))/dot_general | solution.py:11
  445.4 13.4 %fusion.25 = f32[6,1,256,1]{2,1,3,0:T(1,128)S(1)} fusion(f32[2,1024,6,256]{1,3,2,0:T(8,128)} %copy-done.2, f32[6,2,1024,1]{2,0,1,3:T(8,128)S(1)} %bitcast.318), kind=kOutput, calls=%fused_computation.48 | convolution fusion | flops 37748736 | bytes 12638208 | tf_op jit(solution)/shard_map/transpose(jvp(slhn,hn->slh))/dot_general | solution.py:11
  465.3 8.3 fusion.66
  473.6 82.5 %all-reduce.6 = (f32[768]{0:T(1024)S(1)}, f32[768]{0:T(1024)S(1)}, f32[2,384]{1,0:T(2,128)}, f32[2,6,256]{2,1,0:T(8,128)S(1)}, f32[2,6]{1,0:T(2,128)}, /*index=5...) all-reduce(f32[768]{0:T(1024)S(1)} %get-tuple-element.115, ...), channel_id=1, replica_groups=mesh['batch'=16,'mp'=2] {'batch'}, use_global_device_ids=true, to_apply=%region_23.24 | all-reduce | flops 9996 | bytes 79968 | tf_op jit(solution)/shard_map/psum | solution.py:353
  556.7 4.0 all-reduce.8
  560.7 270.3 %all-reduce.11.cloned.1.call-done = (f32[768,3,384]{2,0,1:T(8,128)}, f32[384,768]{1,0:T(8,128)}, f32[768,1536]{1,0:T(8,128)}, f32[1536,768]{1,0:T(8,128)}) async-done(((f32[768,3,384]{2,0,1:T(8,128)}, f32[384,768]{1,0:T(8,128)}, f32[768,1536]{1,0:T(8,128)}, f32[1536,768]{1,0:T(8,128)}), (f32[768,3,384]{2,0,1:T(8,128)}, f32[384,768]{1,0:T(8,128)}, f32[768,1536]{1,0:T(8,128)}, ...) | async-done | bytes 14155792 | tf_op jit(solution)/shard_map/psum | solution.py:332
  831.0 4.2 copy.187
  (303 shorter events, 72.4 us)
Async XLA Ops:
  7.2 153.6 %copy-start = (bf16[768,1536]{1,0:T(8,128)(2,1)S(1)}, bf16[768,1536]{1,0:T(8,128)(2,1)}, u32[]{:S(2)}) copy-start(bf16[768,1536]{1,0:T(8,128)(2,1)} %param.45) | copy-start | bytes 7077892
  7.2 21.4 %all-gather.5.cloned.1.call-start = ((), (), s32[]{:S(2)}) async-start(), calls=%async_computation.5 | async-start | bytes 4718592 | tf_op jit(solution)/shard_map/all_gather | solution.py:264
  13.7 127.4 %reduce-scatter.6.cloned.1.call-start = ((), (), s32[]{:S(2)}) async-start(), calls=%async_computation.6 | async-start | bytes 9437184 | tf_op jit(solution)/shard_map/reduce_scatter | solution.py:277
  20.1 19.1 %copy-start.30 = (bf16[2,256,1,384]{1,3,0,2:T(8,128)(2,1)}, bf16[2,256,1,384]{1,3,0,2:T(8,128)(2,1)S(1)}, u32[]{:S(2)}) copy-start(bf16[2,256,1,384]{1,3,0,2:T(8,128)(2,1)S(1)} %copy.61) | copy-start | bytes 1179652
  21.7 54.1 %copy-start.18 = (pred[512,512]{0,1:T(8,128)(4,1)}, pred[512,512]{0,1:T(8,128)(4,1)S(1)}, u32[]{:S(2)}) copy-start(pred[512,512]{0,1:T(8,128)(4,1)S(1)} %iota_compare_fusion.1) | copy-start | bytes 786436
  25.9 67.4 %copy-start.7 = (pred[512,1024]{1,0:T(8,128)(4,1)}, pred[512,1024]{1,0:T(8,128)(4,1)S(1)}, u32[]{:S(2)}) copy-start(pred[512,1024]{1,0:T(8,128)(4,1)S(1)} %iota_compare_fusion) | copy-start | bytes 1572868
  39.3 17.9 %copy-start.9 = (bf16[2,1024,6,64]{1,3,2,0:T(8,128)(2,1)}, bf16[2,1024,6,64]{1,3,2,0:T(8,128)(2,1)S(1)}, u32[]{:S(2)}) copy-start(bf16[2,1024,6,64]{1,3,2,0:T(8,128)(2,1)S(1)} %add_convert_fusion.3) | copy-start | bytes 4718596
  45.7 56.3 %copy-start.34 = (f32[6,1,2,1024]{3,1,2,0:T(1,128)}, f32[6,1,2,1024]{3,1,2,0:T(1,128)S(1)}, u32[]{:S(2)}) copy-start(f32[6,1,2,1024]{3,1,2,0:T(1,128)S(1)} %fusion.29) | copy-start | bytes 147460
  50.0 51.9 %copy-start.36 = (f32[6,1,2,1024]{3,1,2,0:T(1,128)}, f32[6,1,2,1024]{3,1,2,0:T(1,128)S(1)}, u32[]{:S(2)}) copy-start(f32[6,1,2,1024]{3,1,2,0:T(1,128)S(1)} %fusion.31) | copy-start | bytes 147460
  57.1 10.7 %copy-start.15 = (f32[2,1024,1,384]{1,3,2,0:T(8,128)S(1)}, f32[2,1024,1,384]{1,3,2,0:T(8,128)}, u32[]{:S(2)}) copy-start(f32[2,1024,1,384]{1,3,2,0:T(8,128)} %get-tuple-element.148) | copy-start | bytes 9437188
  68.1 25.2 %copy-start.16 = (bf16[2,1024,6,64]{1,3,2,0:T(8,128)(2,1)}, bf16[2,1024,6,64]{1,3,2,0:T(8,128)(2,1)S(1)}, u32[]{:S(2)}) copy-start(bf16[2,1024,6,64]{1,3,2,0:T(8,128)(2,1)S(1)} %add_convert_fusion.4) | copy-start | bytes 4718596
  68.1 15.5 %slice-start = ((s8[25165824]{0:T(1024)(128)(4,1)}), s8[4194304]{0:T(1024)(128)(4,1)S(1)}, s32[]{:S(2)}) async-start(s8[25165824]{0:T(1024)(128)(4,1)} %bitcast.287), calls=%async_computation.15 | async-start | bytes 8388608
  68.1 15.5 %slice-start.1 = ((s8[25165824]{0:T(1024)(128)(4,1)}), s8[4194304]{0:T(1024)(128)(4,1)S(1)}, s32[]{:S(2)}) async-start(s8[25165824]{0:T(1024)(128)(4,1)} %bitcast.287), calls=%async_computation.16 | async-start | bytes 8388608
  75.9 10.0 %slice-start.5 = ((s8[25165824]{0:T(1024)(128)(4,1)}), s8[4194304]{0:T(1024)(128)(4,1)S(1)}, s32[]{:S(2)}) async-start(s8[25165824]{0:T(1024)(128)(4,1)} %bitcast.287), calls=%async_computation.20 | async-start | bytes 8388608
  93.3 9.5 %copy-start.39 = (bf16[2,256,1,384]{1,3,0,2:T(8,128)(2,1)S(1)}, bf16[2,256,1,384]{1,3,0,2:T(8,128)(2,1)}, u32[]{:S(2)}) copy-start(bf16[2,256,1,384]{1,3,0,2:T(8,128)(2,1)} %copy.60) | copy-start | bytes 1179652
  93.3 9.5 %copy-start.89 = (f32[2]{0:T(128)S(1)}, f32[2]{0:T(128)}, u32[]{:S(2)}) copy-start(f32[2]{0:T(128)} %get-tuple-element.167) | copy-start | bytes 28
  93.3 9.5 %copy-start.90 = (f32[256]{0:T(256)S(1)}, f32[256]{0:T(256)}, u32[]{:S(2)}) copy-start(f32[256]{0:T(256)} %add_multiply_fusion) | copy-start | bytes 3076
  102.0 17.6 %copy-start.57 = (f32[2,1024,6]{1,2,0:T(8,128)}, f32[2,1024,6]{1,2,0:T(8,128)S(1)}, u32[]{:S(2)}) copy-start(f32[2,1024,6]{1,2,0:T(8,128)S(1)} %fusion.189) | copy-start | bytes 147460
  102.8 16.8 %copy-start.53 = (f32[2,1024,6]{1,2,0:T(8,128)}, f32[2,1024,6]{1,2,0:T(8,128)S(1)}, u32[]{:S(2)}) copy-start(f32[2,1024,6]{1,2,0:T(8,128)S(1)} %get-tuple-element.157) | copy-start | bytes 147460
  102.8 16.8 %copy-start.55 = (f32[2,1024,6]{1,2,0:T(8,128)}, f32[2,1024,6]{1,2,0:T(8,128)S(1)}, u32[]{:S(2)}) copy-start(f32[2,1024,6]{1,2,0:T(8,128)S(1)} %get-tuple-element.155) | copy-start | bytes 147460
  102.8 18.0 %copy-start.38 = (bf16[384,768]{1,0:T(8,128)(2,1)S(1)}, bf16[384,768]{1,0:T(8,128)(2,1)}, u32[]{:S(2)}) copy-start(bf16[384,768]{1,0:T(8,128)(2,1)} %param.41) | copy-start | bytes 1769476
  125.2 15.9 %copy-start.79 = (f32[768]{0:T(1024)S(1)}, f32[768]{0:T(1024)}, u32[]{:S(2)}) copy-start(f32[768]{0:T(1024)} %param.42) | copy-start | bytes 9220
  125.2 35.6 %all-gather.7.cloned.1.call-start = ((), (), s32[]{:S(2)}) async-start(), calls=%async_computation.7 | async-start | bytes 4718592 | tf_op jit(solution)/shard_map/all_gather | solution.py:280
  144.0 79.1 %copy-start.44 = (f32[2,512]{1,0:T(2,128)}, f32[2,512]{1,0:T(2,128)S(1)}, u32[]{:S(2)}) copy-start(f32[2,512]{1,0:T(2,128)S(1)} %broadcast_multiply_fusion.6) | copy-start | bytes 12292
  145.6 77.4 %copy-start.48 = (f32[2,512]{1,0:T(2,128)}, f32[2,512]{1,0:T(2,128)S(1)}, u32[]{:S(2)}) copy-start(f32[2,512]{1,0:T(2,128)S(1)} %add_rsqrt_fusion) | copy-start | bytes 12292
  147.3 28.2 %all-gather.9.cloned.1.call-start = ((), (), s32[]{:S(2)}) async-start(), calls=%async_computation.9 | async-start | bytes 4718592 | tf_op jit(solution)/shard_map/all_gather | solution.py:288
  147.9 70.4 %reduce-scatter.10.cloned.1.call-start = ((), (), s32[]{:S(2)}) async-start(), calls=%async_computation.10 | async-start | bytes 9437184 | tf_op jit(solution)/shard_map/reduce_scatter | solution.py:292
  202.5 20.6 %copy-start.14 = (bf16[2,512,768]{2,1,0:T(8,128)(2,1)S(1)}, bf16[2,512,768]{2,1,0:T(8,128)(2,1)}, u32[]{:S(2)}) copy-start(bf16[2,512,768]{2,1,0:T(8,128)(2,1)} %param.49) | copy-start | bytes 4718596
  202.5 38.3 %all-gather.11.cloned.1.call-start = ((), (), s32[]{:S(2)}) async-start(), calls=%async_computation.11 | async-start | bytes 4718592 | tf_op jit(solution)/shard_map/all_gather | solution.py:300
  227.4 233.1 %reduce-scatter.14.cloned.1.call-start = ((), (), s32[]{:S(2)}) async-start(), calls=%async_computation.13 | async-start | bytes 1179648 | tf_op jit(solution)/shard_map/reduce_scatter | solution.py:316
  227.5 16.8 %copy-start.19 = (pred[512,512]{0,1:T(8,128)(4,1)S(1)}, pred[512,512]{0,1:T(8,128)(4,1)}, u32[]{:S(2)}) copy-start(pred[512,512]{0,1:T(8,128)(4,1)} %copy-done.18) | copy-start | bytes 786436
  240.8 11.5 %slice-start.6 = ((s8[12582912]{0:T(1024)(128)(4,1)}), s8[4194304]{0:T(1024)(128)(4,1)S(1)}, s32[]{:S(2)}) async-start(s8[12582912]{0:T(1024)(128)(4,1)} %bitcast.289), calls=%async_computation.21 | async-start | bytes 8388608
  244.3 28.1 %copy-start.32 = (bf16[2,1024,384]{1,2,0:T(8,128)(2,1)}, bf16[2,1024,384]{1,2,0:T(8,128)(2,1)S(1)}, u32[]{:S(2)}) copy-start(bf16[2,1024,384]{1,2,0:T(8,128)(2,1)S(1)} %convolution_convert_fusion) | copy-start | bytes 4718596
  276.7 11.4 %copy-start.35 = (f32[6,1,2,1024]{3,1,2,0:T(1,128)S(1)}, f32[6,1,2,1024]{3,1,2,0:T(1,128)}, u32[]{:S(2)}) copy-start(f32[6,1,2,1024]{3,1,2,0:T(1,128)} %copy-done.34) | copy-start | bytes 147460
  276.7 11.4 %copy-start.37 = (f32[6,1,2,1024]{3,1,2,0:T(1,128)S(1)}, f32[6,1,2,1024]{3,1,2,0:T(1,128)}, u32[]{:S(2)}) copy-start(f32[6,1,2,1024]{3,1,2,0:T(1,128)} %copy-done.36) | copy-start | bytes 147460
  276.7 11.4 %copy-start.72 = (f32[6]{0:T(128)S(1)}, f32[6]{0:T(128)}, u32[]{:S(2)}) copy-start(f32[6]{0:T(128)} %get-tuple-element.164) | copy-start | bytes 76
  276.7 11.4 %copy-start.74 = (f32[6]{0:T(128)S(1)}, f32[6]{0:T(128)}, u32[]{:S(2)}) copy-start(f32[6]{0:T(128)} %get-tuple-element.165) | copy-start | bytes 76
  276.7 11.6 %copy-start.75 = (f32[6,256]{1,0:T(8,128)S(1)}, f32[6,256]{1,0:T(8,128)}, u32[]{:S(2)}) copy-start(f32[6,256]{1,0:T(8,128)} %get-tuple-element.160) | copy-start | bytes 18436
  276.7 11.6 %copy-start.76 = (f32[6,256]{1,0:T(8,128)S(1)}, f32[6,256]{1,0:T(8,128)}, u32[]{:S(2)}) copy-start(f32[6,256]{1,0:T(8,128)} %get-tuple-element.158) | copy-start | bytes 18436
  288.3 73.9 %copy-start.42 = (f32[6,2,1024]{2,0,1:T(8,128)}, f32[6,2,1024]{2,0,1:T(8,128)S(1)}, u32[]{:S(2)}) copy-start(f32[6,2,1024]{2,0,1:T(8,128)S(1)} %get-tuple-element.180) | copy-start | bytes 147460
  297.9 164.5 %reduce-scatter.12.cloned.1.call-start = ((), (), s32[]{:S(2)}) async-start(), calls=%async_computation.12 | async-start | bytes 4718592 | tf_op jit(solution)/shard_map/reduce_scatter | solution.py:313
  332.1 21.4 %copy-start.13 = (bf16[2,1024,1,384]{1,3,2,0:T(8,128)(2,1)S(1)}, bf16[2,1024,1,384]{1,3,2,0:T(8,128)(2,1)}, u32[]{:S(2)}) copy-start(bf16[2,1024,1,384]{1,3,2,0:T(8,128)(2,1)} %slice.267) | copy-start | bytes 4718596
  390.2 75.1 %reduce-scatter.8.cloned.1.call-start = ((), (), s32[]{:S(2)}) async-start(), calls=%async_computation.8 | async-start | bytes 4718592 | tf_op jit(solution)/shard_map/reduce_scatter | solution.py:284
  399.3 431.7 %all-reduce.11.cloned.1.call-start = ((), (), s32[]{:S(2)}) async-start(), calls=%async_computation.14 | async-start | bytes 28311552 | tf_op jit(solution)/shard_map/psum | solution.py:332
  399.4 10.4 %copy-start.85 = (bf16[2,1024,768]{2,1,0:T(8,128)(2,1)S(1)}, bf16[2,1024,768]{2,1,0:T(8,128)(2,1)}, u32[]{:S(2)}) copy-start(bf16[2,1024,768]{2,1,0:T(8,128)(2,1)} %all-gather.9.cloned.1.call-done) | copy-start | bytes 9437188
  409.7 8.9 %copy-start.23 = (bf16[2,1024,1,384]{3,1,2,0:T(8,128)(2,1)S(1)}, bf16[2,1024,1,384]{3,1,2,0:T(8,128)(2,1)}, u32[]{:S(2)}) copy-start(bf16[2,1024,1,384]{3,1,2,0:T(8,128)(2,1)} %copy.70) | copy-start | bytes 4718596
  445.4 13.7 %copy-start.22 = (bf16[2,1024,1,384]{3,1,2,0:T(8,128)(2,1)S(1)}, bf16[2,1024,1,384]{3,1,2,0:T(8,128)(2,1)}, u32[]{:S(2)}) copy-start(bf16[2,1024,1,384]{3,1,2,0:T(8,128)(2,1)} %copy.69) | copy-start | bytes 4718596
  445.4 13.7 %copy-start.24 = (bf16[2,1024,1,384]{3,1,2,0:T(8,128)(2,1)S(1)}, bf16[2,1024,1,384]{3,1,2,0:T(8,128)(2,1)}, u32[]{:S(2)}) copy-start(bf16[2,1024,1,384]{3,1,2,0:T(8,128)(2,1)} %copy.70) | copy-start | bytes 4718596
  (67 other events, 331.0 us)
Sparse Core Ops, SparseCore 0:
  13.8 14.8 all-gather.4
  125.3 15.6 reduce-scatter.5
  147.5 13.2 all-gather.6
  162.3 13.2 all-gather.8
  202.6 15.6 reduce-scatter.9
  227.5 13.2 all-gather.10
  298.0 9.4 reduce-scatter.13
  390.3 12.0 reduce-scatter.11
  404.7 12.0 reduce-scatter.7
  431.3 399.6 all-reduce.10
